TPU v7x, 32 devices: a whole 2x2x4 slice. The times are simulated.
32 devices in a mesh: dp: 4 (over x, core), ctx: 8 (over z, y).
Axes of the slice: x: 2, y: 2, z: 4, core: 2. Of those that a mesh axis runs over, the one named last changes fastest.
Arguments:
- qkv: bfloat16 [4, 3, 4096, 1024], P('dp', None, None, 'ctx'), may hold values from -6 to 6
- taps: float32 [3, 3, 4096], P(None, None, 'ctx'), may hold values from -3.5 to 3.5
- rate_table: float32 [16, 4096], P('dp', 'ctx'), may hold values from 0.00029296875 to 2, as said below
- residue_table: float32 [16, 4096], P('dp', 'ctx'), may hold values from -5 to 5
- bias: float32 [4096], P('ctx'), may hold values from -0.5 to 0.5
Outputs:
- mixed: bfloat16 [4, 4096, 1024], P('dp', None, 'ctx')
Inputs may be any that keep to these rules, and one draw needn't show every extreme that they name: `rate_table`: every rate is positive.
All inputs are finite; a program needn't handle non-finite values.
Results may differ from a plain program's by a relative error of at most 0.0085.
Values may be sent and summed in bfloat16 or wider, within the bound.
A program may use at most 320 MiB of HBM per device.

v0:
```python
import jax
import jax.numpy as jnp
from jax import lax
from jax.sharding import PartitionSpec as P

ORDER = 16


def combine(earlier, later):
    return (earlier[0] * later[0], earlier[1] * later[0] + later[1])


def short_filter(extended, taps):
    now = extended[..., 2:]
    one_back = extended[..., 1:-1]
    two_back = extended[..., :-2]
    return (
        taps[0][:, :, None] * now + taps[1][:, :, None] * one_back + taps[2][:, :, None] * two_back
    )


def short_pair(extended, taps):
    signal = extended.astype(jnp.float32)
    filtered = short_filter(signal, taps)
    query = filtered[:, 0]
    gated = (filtered[:, 1] * filtered[:, 2]).astype(jnp.bfloat16)
    return (query, gated)


def toeplitz_block(kernel, width):
    chans = kernel.shape[0]
    blank = jnp.zeros((chans, width + 1), jnp.float32)
    period = jnp.concatenate([kernel[:, :1], blank, kernel[:, :0:-1]], axis=1)
    repeated = jnp.tile(period, (1, width))
    skewed = repeated[:, : 2 * width * width].reshape(chans, width, 2 * width)
    return skewed[:, :, :width]


def block_terms(signal, rate, coef, width):
    precise = lax.Precision.HIGHEST
    lag = jnp.arange(width).astype(jnp.float32)
    decay = jnp.exp(-rate[:, :, None] * lag)
    kernel = jnp.einsum("nc,ncb->cb", coef, decay, precision=precise)
    toeplitz = toeplitz_block(kernel, width)
    inner = jnp.einsum("cts,cks->ckt", toeplitz, signal, precision=precise)
    tail = jnp.exp(-rate[:, :, None] * (width - 1.0 - lag))
    states = jnp.einsum("ncs,cks->cnk", tail, signal, precision=precise)
    return (inner, states)


def carried(incoming, rate, coef, width):
    lag = jnp.arange(width).astype(jnp.float32)
    head = coef[:, :, None] * jnp.exp(-rate[:, :, None] * (lag + 1.0))
    return jnp.einsum("ncb,cnk->ckb", head, incoming, precision=lax.Precision.HIGHEST)


def blocked_conv(signal_flat, rate, coef, start_state):
    chans, length = signal_flat.shape
    width = min(128, length)
    count = length // width
    signal = signal_flat.reshape(chans, count, width)
    inner, states = block_terms(signal, rate, coef, width)
    block_decay = jnp.broadcast_to(jnp.exp(-rate * width).T[:, :, None], states.shape)
    _, prefix = lax.associative_scan(combine, (block_decay, states), axis=2)
    incoming = jnp.concatenate([jnp.zeros_like(prefix[:, :, :1]), prefix[:, :, :-1]], axis=2)
    start_lag = jnp.arange(count).astype(jnp.float32) * width
    incoming = incoming + start_state[:, :, None] * jnp.exp(-rate.T[:, :, None] * start_lag)
    conv = (inner + carried(incoming, rate, coef, width)).reshape(chans, length)
    last = prefix[:, :, -1]
    return (conv, last)


def channel_long(gated, rate, coef, bias):
    signal = gated.astype(jnp.float32)
    start = jnp.zeros((signal.shape[0], rate.shape[0]), jnp.float32)
    conv, _ = blocked_conv(signal, rate, coef, start)
    return (conv + bias[:, None] * signal).astype(jnp.bfloat16)


def per_device(qkv, taps, rate_table, residue_table, bias):
    rate, residue = (
        lax.all_gather(rate_table, "dp", axis=0, tiled=True),
        lax.all_gather(residue_table, "dp", axis=0, tiled=True),
    )
    coef = residue * jnp.sqrt(2.0 * rate / ORDER)
    extended = jnp.pad(
        lax.all_to_all(qkv, "ctx", split_axis=2, concat_axis=3, tiled=True),
        ((0, 0), (0, 0), (0, 0), (2, 0)),
    )
    query, gated = short_pair(extended, taps)
    long = jax.vmap(lambda single: channel_long(single, rate, coef, bias))(gated)
    regrouped = (query * long.astype(jnp.float32)).astype(jnp.bfloat16)
    return lax.all_to_all(regrouped, "ctx", split_axis=2, concat_axis=1, tiled=True)


def solution(mesh):
    in_specs = (
        P("dp", None, None, "ctx"),
        P(None, None, "ctx"),
        P("dp", "ctx"),
        P("dp", "ctx"),
        P("ctx"),
    )
    out_specs = P("dp", None, "ctx")
    return jax.shard_map(
        per_device, mesh=mesh, in_specs=in_specs, out_specs=out_specs, check_vma=False
    )
```

profile of v0, /device:TPU:24, one launch (start us, length us, event | category | flops | bytes accessed | tf_op | source)
XLA Modules:
  0.0 348.5 jit_solution(4426221832621744879)
XLA Ops:
  0.0 6.8 %copy.87 = bf16[1,3,4096,128]{3,1,0,2:T(4,128)(2,1)} copy(bf16[1,3,4096,128]{3,2,1,0:T(8,128)(2,1)} %param.5) | data formatting | bytes 6291456 | tf_op args[0]
  6.8 6.2 %all-to-all-start = ((bf16[1,3,4096,128]{3,1,0,2:T(4,128)(2,1)}), bf16[1,3,4096,128]{3,1,0,2:T(4,128)(2,1)}, u32[]{:S(2)}, u32[]{:S(2)}) async-start(bf16[1,3,4096,128]{3,1,0,2:T(4,128)(2,1)} %copy.87), calls=%async_computation | async-start | bytes 8388608 | tf_op jit(solution)/shard_map/all_to_all | solution.py:87
  13.0 5.2 %all-gather.1 = f32[4,4,512]{2,1,0:T(4,128)S(1)} all-gather(f32[1,4,512]{2,1,0:T(4,128)S(1)} %bitcast.85), channel_id=1, replica_groups=mesh['dp'=4,'ctx'=8] {'dp'}, dimensions={0}, use_global_device_ids=true | all-gather | bytes 40960 | tf_op jit(solution)/shard_map/all_gather | solution.py:82
  18.1 5.2 %all-gather = f32[4,4,512]{2,1,0:T(4,128)S(1)} all-gather(f32[1,4,512]{2,1,0:T(4,128)S(1)} %bitcast.86), channel_id=1, replica_groups=mesh['dp'=4,'ctx'=8] {'dp'}, dimensions={0}, use_global_device_ids=true | all-gather | bytes 40960 | tf_op jit(solution)/shard_map/all_gather | solution.py:83
  24.5 6.0 %multiply_reduce_fusion = f32[512,128]{1,0:T(8,128)S(1)} fusion(f32[512,16]{1,0:T(8,128)S(1)} %copy.107, f32[128]{0:T(128)S(1)} %iota_convert_fusion, f32[16,512]{0,1:T(8,128)S(1)} %copy.89), kind=kLoop, calls=%fused_computation.5 | loop fusion | flops 3080192 | bytes 328192
  31.3 22.1 %tile.4 = f32[512,128,257]{0,2,1:T(8,128)} broadcast(f32[512,257]{0,1:T(8,128)S(1)} %pad_maximum_fusion), dimensions={0,2} | broadcast | bytes 67897344 | tf_op jit(solution)/shard_map/vmap()/tile | solution.py:34
  53.4 78.8 %tile.10 = f32[512,32896]{0,1:T(8,128)} reshape(f32[512,128,257]{0,2,1:T(8,128)} %tile.4) | data formatting | bytes 134742016 | tf_op jit(solution)/shard_map/vmap()/tile | solution.py:34
  132.2 43.2 %slice.123 = f32[512,32768]{0,1:T(8,128)} slice(f32[512,32896]{0,1:T(8,128)} %tile.10), slice={[0:512], [0:32768]} | slice | bytes 134217728 | tf_op jit(solution)/shard_map/vmap()/slice | solution.py:35
  175.5 23.5 %slice.124 = f32[512,128,128]{0,2,1:T(8,128)} slice(f32[512,128,256]{0,2,1:T(8,128)} %bitcast.10), slice={[0:512], [0:128], [0:128]} | slice | bytes 67108864 | tf_op jit(solution)/shard_map/vmap()/slice | solution.py:36
  199.0 35.6 %copy.106 = f32[512,128,128]{2,1,0:T(8,128)} copy(f32[512,128,128]{0,2,1:T(8,128)} %slice.124) | data formatting | bytes 67108864
  234.7 4.8 %copy.110 = bf16[1,3,8,512,128]{4,2,3,1,0:T(8,128)(2,1)S(1)} copy(bf16[1,3,8,512,128]{4,1,3,2,0:T(4,128)(2,1)} %bitcast.3) | data formatting | bytes 6291456 | tf_op jit(solution)/shard_map/all_to_all | solution.py:87
  239.4 3.4 all_to_all.29
  242.8 3.3 pad_convert_fusion
  246.1 5.2 %fusion = f32[1,3,512,1024]{3,2,1,0:T(8,128)S(1)} fusion(f32[1,3,512,1026]{3,2,1,0:T(8,128)S(1)} %pad_convert_fusion, f32[3,512]{1,0:T(4,128)S(1)} %get-tuple-element.12, f32[3,512]{1,0:T(4,128)S(1)} %get-tuple-element.13, f32[3,512]{1,0:T(4,128)S(1)} %get-tuple-element.11), kind=kLoop, calls=%fused_computation.1 | loop fusion | flops 7864320 | bytes 25184256 | tf_op jit(solution)/shard_map/add | solution.py:18
  251.3 2.6 copy-done
  254.7 3.7 %fusion.6 = f32[512,16,8]{1,2,0:T(8,128)S(1)} fusion(bf16[512,8,128]{2,1,0:T(8,128)(2,1)S(1)} %bitcast.76, f32[128]{0:T(128)S(1)} %broadcast_subtract_fusion, f32[16,512]{0,1:T(8,128)S(1)} %copy.89), kind=kOutput, calls=%fused_computation.10 | convolution fusion | flops 101711872 | bytes 1344000 | tf_op jit(solution)/shard_map/vmap(ncs,cks->cnk)/dot_general | solution.py:47
  260.0 29.8 %fusion.29 = f32[512,8,128]{2,1,0:T(8,128)S(1)} fusion(bf16[512,8,128]{2,1,0:T(8,128)(2,1)S(1)} %bitcast.77, f32[512,128,128]{2,1,0:T(8,128)} %copy.106), kind=kOutput, calls=%fused_computation.60 | convolution fusion | flops 805306368 | bytes 36700160 | tf_op jit(solution)/shard_map/vmap(cts,cks->ckt)/dot_general | solution.py:45
  291.6 2.0 copy.93
  293.6 7.7 %fusion.19 = f32[512,8,128]{2,1,0:T(8,128)} fusion(f32[512,8,128]{2,1,0:T(8,128)S(1)} %fusion.29, f32[512,16,8]{1,2,0:T(8,128)} %copy.93, f32[128]{0:T(128)S(1)} %broadcast_add_fusion, f32[16,512]{0,1:T(8,128)S(1)} %copy-done.1, f32[16,512]{0,1:T(8,128)S(1)} %copy-done.3), kind=kOutput, calls=%fused_computation.28 | convolution fusion | flops 103284736 | bytes 4522496 | tf_op jit(solution)/shard_map/vmap(ncb,cnk->ckb)/dot_general | solution.py:54
  301.3 1.7 transpose.40
  303.0 3.3 fusion.11
  306.3 1.8 copy.94
  308.7 7.0 %reduce.2 = bf16[1024,512]{1,0:T(8,128)(2,1)S(1)} reduce(bf16[1024,1,512]{2,1,0:T(2,128)(2,1)S(1)} %bitcast.75, bf16[]{:T(256)} %broadcast.111), dimensions={1}, to_apply=%bitcast.64.reduce_sub_computation | reduce | bytes 2097154
  316.5 29.4 %all_to_all.36 = bf16[8,2,32768]{2,1,0:T(2,128)(2,1)S(1)} all-to-all(bf16[8,2,32768]{2,1,0:T(2,128)(2,1)S(1)} %reshape.203), channel_id=1, replica_groups=mesh['dp'=4,'ctx'=8] {'ctx'}, dimensions={0} | all-to-all | bytes 2097152 | tf_op jit(solution)/shard_map/all_to_all | solution.py:93
  (60 shorter events, 10.0 us)
Async XLA Ops:
  6.8 6.2 %copy-start.5 = (f32[4,512]{1,0:T(4,128)S(1)}, f32[4,512]{1,0:T(4,128)}, u32[]{:S(2)}) copy-start(f32[4,512]{1,0:T(4,128)} %param.7) | copy-start | bytes 24580
  6.8 11.4 %copy-start.6 = (f32[4,512]{1,0:T(4,128)S(1)}, f32[4,512]{1,0:T(4,128)}, u32[]{:S(2)}) copy-start(f32[4,512]{1,0:T(4,128)} %param.8) | copy-start | bytes 24580
  6.8 227.9 %all-to-all-start = ((bf16[1,3,4096,128]{3,1,0,2:T(4,128)(2,1)}), bf16[1,3,4096,128]{3,1,0,2:T(4,128)(2,1)}, u32[]{:S(2)}, u32[]{:S(2)}) async-start(bf16[1,3,4096,128]{3,1,0,2:T(4,128)(2,1)} %copy.87), calls=%async_computation | async-start | bytes 8388608 | tf_op jit(solution)/shard_map/all_to_all | solution.py:87
  24.5 230.2 %copy-start.2 = (f32[16,512]{0,1:T(8,128)}, f32[16,512]{0,1:T(8,128)S(1)}, u32[]{:S(2)}) copy-start(f32[16,512]{0,1:T(8,128)S(1)} %copy.89) | copy-start | bytes 98308
  199.0 35.6 %copy-start.4 = (f32[3,3,512]{2,1,0:T(4,128)S(1)}, f32[3,3,512]{2,1,0:T(4,128)}, u32[]{:S(2)}) copy-start(f32[3,3,512]{2,1,0:T(4,128)} %param.6) | copy-start | bytes 55300
  251.3 2.6 copy-start
  289.8 3.8 %copy-start.1 = (f32[16,512]{0,1:T(8,128)S(1)}, f32[16,512]{0,1:T(8,128)}, u32[]{:S(2)}) copy-start(f32[16,512]{0,1:T(8,128)} %copy.92) | copy-start | bytes 98308
  289.8 3.8 %copy-start.3 = (f32[16,512]{0,1:T(8,128)S(1)}, f32[16,512]{0,1:T(8,128)}, u32[]{:S(2)}) copy-start(f32[16,512]{0,1:T(8,128)} %copy-done.2) | copy-start | bytes 98308
  293.6 9.5 %copy-start.7 = (f32[512]{0:T(512)S(1)}, f32[512]{0:T(512)}, u32[]{:S(2)}) copy-start(f32[512]{0:T(512)} %param.9) | copy-start | bytes 6148
where the time goes:
time: 354 us; the launch traced here: 349 us
  local copies, waits for them, and re-layouts  235 us (66%)
  matrix products  41.2 us (12%)
  blocking collectives  39.7 us (11%)
  other arithmetic  26.4 us (7%)
  starting transfers between devices  6.19 us (2%)
    another operation x2, local copies, waits for them, and re-layouts, toeplitz_block(): repeated = jnp.tile(period, (1, width))  101 us
    unnamed x27, local copies, waits for them, and re-layouts  49.9 us
    slice x1, local copies, waits for them, and re-layouts, toeplitz_block(): skewed = repeated[:, :2 * width * width].reshape(chans, width, 2 * width)  43.2 us
    dot_general x1, matrix products, block_terms(): inner = jnp.einsum('cts,cks->ckt', toeplitz, signal, precision=precise)  29.8 us
    all_to_all x1, blocking collectives, per_device(): lax.all_to_all(regrouped, 'ctx', split_axis=2, concat_axis=1, tiled=True)  29.4 us
    slice x1, local copies, waits for them, and re-layouts, toeplitz_block(): return skewed[:, :, :width]  23.5 us
    unnamed x3, other arithmetic  13.5 us
    all_to_all x2, local copies, waits for them, and re-layouts, per_device(): lax.all_to_all(qkv, 'ctx', split_axis=2, concat_axis=3, tiled=True)  8.1 us
  transfers between devices with their start and end apart: 1, of which 0 were waited for; matrix products, arithmetic and copies ran while one was open for 61% of the time, Pallas kernels for 0%

commit v1 on v0

v1 whole, which is shorter than its diff:
```python
import functools
import jax
import jax.numpy as jnp
from jax import lax
from jax.experimental import pallas as pl
from jax.experimental.pallas import tpu as pltpu
from jax.sharding import PartitionSpec as P

ORDER = 16
LANES = 128
SUB = 8
GROUP = LANES * SUB


def identity(size):
    rows = lax.broadcasted_iota(jnp.int32, (size, size), 0)
    columns = lax.broadcasted_iota(jnp.int32, (size, size), 1)
    return (rows == columns).astype(jnp.bfloat16)


def flipped(eye, block):
    return lax.dot_general(
        eye, block, (((1,), (1,)), ((), ())), preferred_element_type=jnp.float32
    )


def to_tokens(eye, source, target, blocks, group, tokens):
    for sub in range(SUB):
        block = group * SUB + sub
        tile = source[pl.ds(pl.multiple_of(block * LANES, LANES), LANES), :]
        target[pl.ds(2 * blocks + block, tokens, stride=blocks), :] = flipped(eye, tile)


def rows_at(ref, token, blocks, group):
    return ref[pl.ds(pl.multiple_of(token * blocks + group * SUB, SUB), SUB), :]


def rounded(value):
    return value.astype(jnp.bfloat16).astype(jnp.float32)


def tree_sum(terms):
    terms = list(terms)
    while len(terms) > 1:
        terms = [a + b for a, b in zip(terms[::2], terms[1::2])]
    return terms[0]


def local_kernel(blocks, tokens, kv, halo, taps, bias, decay, coef, y_ref, s_ref, k_s, v_s):
    eye = identity(tokens)
    k_s[0 : 2 * blocks, :] = halo[1]
    v_s[0 : 2 * blocks, :] = halo[2]

    def one_group(group, _):
        to_tokens(eye, kv.at[1], k_s, blocks, group, tokens)
        to_tokens(eye, kv.at[2], v_s, blocks, group, tokens)
        own = pl.ds(pl.multiple_of(group * SUB, SUB), SUB)
        tap = [[taps[i, w, own, :] for i in range(3)] for w in (1, 2)]
        direct = bias[own, :]
        dec = [decay[n, own, :] for n in range(ORDER)]
        coe = [coef[n, own, :] for n in range(ORDER)]

        def step(t, carry):
            k2, k1, v2, v1, states = carry
            k0 = rows_at(k_s, t + 2, blocks, group)
            v0 = rows_at(v_s, t + 2, blocks, group)
            fk = tap[0][0] * k0 + tap[0][1] * k1 + tap[0][2] * k2
            fv = tap[1][0] * v0 + tap[1][1] * v1 + tap[1][2] * v2
            u = rounded(fk * fv)
            states = tuple(d * s + u for d, s in zip(dec, states))
            y = tree_sum(c * s for c, s in zip(coe, states)) + direct * u
            y_ref[pl.ds(pl.multiple_of(t * blocks + group * SUB, SUB), SUB), :] = y
            return (k1, k0, v1, v0, states)

        zero = jnp.zeros((SUB, LANES), jnp.float32)
        start = (
            rows_at(k_s, 0, blocks, group),
            rows_at(k_s, 1, blocks, group),
            rows_at(v_s, 0, blocks, group),
            rows_at(v_s, 1, blocks, group),
            (zero,) * ORDER,
        )
        states = lax.fori_loop(0, tokens, step, start, unroll=4)[4]
        for n in range(ORDER):
            s_ref[n, own, :] = states[n]
        return 0

    lax.fori_loop(0, blocks // SUB, one_group, 0)


def final_kernel(blocks, tokens, qkv, halo, taps, decay, coef, carry, y_ref, out, q_s):
    eye = identity(tokens)
    q_s[0 : 2 * blocks, :] = halo[0]

    def one_group(group, _):
        to_tokens(eye, qkv.at[0], q_s, blocks, group, tokens)
        own = pl.ds(pl.multiple_of(group * SUB, SUB), SUB)
        tap = [taps[i, 0, own, :] for i in range(3)]
        dec = [decay[n, own, :] for n in range(ORDER)]
        first = tuple(coef[n, own, :] * carry[n, own, :] for n in range(ORDER))

        def step(t, state):
            q2, q1, parts = state
            q0 = rows_at(q_s, t + 2, blocks, group)
            parts = tuple(d * z for d, z in zip(dec, parts))
            long = rounded(rows_at(y_ref, t, blocks, group) + tree_sum(parts))
            fq = tap[0] * q0 + tap[1] * q1 + tap[2] * q2
            q_s[pl.ds(pl.multiple_of(t * blocks + group * SUB, SUB), SUB), :] = fq * long
            return (q1, q0, parts)

        lax.fori_loop(
            0,
            tokens,
            step,
            (rows_at(q_s, 0, blocks, group), rows_at(q_s, 1, blocks, group), first),
            unroll=4,
        )
        for sub in range(SUB):
            block = group * SUB + sub
            tile = q_s[pl.ds(block, tokens, stride=blocks), :].astype(jnp.bfloat16)
            out[pl.ds(pl.multiple_of(block * LANES, LANES), LANES), :] = flipped(eye, tile).astype(
                jnp.bfloat16
            )
        return 0

    lax.fori_loop(0, blocks // SUB, one_group, 0)


def gathered(taps, rate_table, residue_table, bias, dp, ctx):
    modes, width = rate_table.shape
    rows = -(-10 // dp)
    extra = jnp.concatenate(
        [taps.reshape(9, width), bias[None], jnp.zeros((rows * dp - 10, width), jnp.float32)]
    )
    own = lax.dynamic_slice_in_dim(extra, lax.axis_index("dp") * rows, rows, 0)
    packed = jnp.concatenate([rate_table, residue_table, own])
    whole = lax.all_gather(packed, ("dp", "ctx"), axis=0)
    height = 2 * modes + rows
    whole = whole.reshape(dp, ctx, height, width).transpose(0, 2, 1, 3)
    whole = whole.reshape(dp, height, ctx * width // LANES, LANES)
    blocks = whole.shape[2]
    rate = whole[:, :modes].reshape(dp * modes, blocks, LANES)
    residue = whole[:, modes : 2 * modes].reshape(dp * modes, blocks, LANES)
    rest = whole[:, 2 * modes :].reshape(dp * rows, blocks, LANES)
    return rate, residue, rest[:9].reshape(3, 3, blocks, LANES), rest[9]


def per_device(dp, ctx, qkv, taps, rate_table, residue_table, bias):
    _, _, chans, tokens = qkv.shape
    blocks = chans // LANES
    own = qkv[0]
    halo = jnp.transpose(own[:, :, tokens - 2 :], (0, 2, 1)).reshape(3, 2 * blocks, LANES)
    halo = lax.ppermute(halo, "ctx", [(i, i + 1) for i in range(ctx - 1)]).astype(jnp.float32)
    rate, residue, taps, bias = gathered(taps, rate_table, residue_table, bias, dp, ctx)
    coef = residue * jnp.sqrt(2.0 * rate / ORDER)
    decay = jnp.exp(-rate)
    vmem = pl.BlockSpec(memory_space=pltpu.VMEM)
    params = pltpu.CompilerParams(vmem_limit_bytes=40 * 1024 * 1024)
    wide = (tokens + 2) * blocks
    y, last = pl.pallas_call(
        functools.partial(local_kernel, blocks, tokens),
        out_shape=(
            jax.ShapeDtypeStruct((tokens * blocks, LANES), jnp.float32),
            jax.ShapeDtypeStruct((ORDER, blocks, LANES), jnp.float32),
        ),
        in_specs=[vmem] * 6,
        out_specs=(vmem, vmem),
        scratch_shapes=[pltpu.VMEM((wide, LANES), jnp.float32)] * 2,
        compiler_params=params,
    )(own, halo, taps, bias, decay, coef)

    block_decay = jnp.exp(-rate * tokens)
    carry = jnp.zeros_like(last)
    reach = 1
    while reach < ctx:
        window = last + block_decay * carry if reach > 1 else last
        moved = lax.ppermute(window, "ctx", [(i, i + reach) for i in range(ctx - reach)])
        carry = carry + jnp.exp(-rate * (tokens * (reach - 1.0))) * moved
        reach *= 2

    out = pl.pallas_call(
        functools.partial(final_kernel, blocks, tokens),
        out_shape=jax.ShapeDtypeStruct((chans, tokens), jnp.bfloat16),
        in_specs=[vmem] * 7,
        out_specs=vmem,
        scratch_shapes=[pltpu.VMEM((wide, LANES), jnp.float32)],
        compiler_params=params,
    )(own, halo, taps, decay, coef, carry, y)
    return out[None]


def solution(mesh):
    in_specs = (
        P("dp", None, None, "ctx"),
        P(None, None, "ctx"),
        P("dp", "ctx"),
        P("dp", "ctx"),
        P("ctx"),
    )
    return jax.shard_map(
        functools.partial(per_device, mesh.shape["dp"], mesh.shape["ctx"]),
        mesh=mesh,
        in_specs=in_specs,
        out_specs=P("dp", None, "ctx"),
        check_vma=False,
    )
```

time: 354 us -> 137 us (0.39); the launches traced: 349 us -> 137 us
  local copies, waits for them, and re-layouts: 235 us -> 9.49 us
  matrix products: 41.2 us -> 0 us
  waiting for transfers between devices: 0.01 us -> 32.2 us
  other arithmetic: 26.4 us -> 1.68 us
  blocking collectives: 39.7 us -> 63.6 us
  Pallas kernels: 0 us -> 20.1 us
    another operation x3 -> x0, local copies, waits for them, and re-layouts: 103 us -> none  [the longest x2 101 us: toeplitz_block(): repeated = jnp.tile(period, (1, width))]
    slice x4 -> x2, local copies, waits for them, and re-layouts: 66.9 us -> 1.87 us  [the longest x1 0.94 us: gathered(): rest = whole[:, 2 * modes:].reshape(dp * rows, blocks, LANES)]
    all_gather x2 -> x1, blocking collectives: 10.4 us -> 63.6 us  [gathered(): whole = lax.all_gather(packed, ('dp', 'ctx'), axis=0)]
    unnamed x27 -> x10, local copies, waits for them, and re-layouts: 49.9 us -> 0.03 us
    dot_general x3 -> x0, matrix products: 41.2 us -> none  [the longest x1 29.8 us: block_terms(): inner = jnp.einsum('cts,cks->ckt', toeplitz, signal, precision=precise)]
    ppermute x0 -> x4, waiting for transfers between devices: none -> 32.2 us  [the longest x3 32.1 us: per_device(): lax.ppermute(window, 'ctx', [(i, i + reach) for i in range(ctx - reach)])]
    all_to_all x1 -> x0, blocking collectives: 29.4 us -> none  [per_device(): lax.all_to_all(regrouped, 'ctx', split_axis=2, concat_axis=1, tiled=True)]
    pallas_call x0 -> x2, Pallas kernels: none -> 20.1 us  [the longest x1 11.2 us: per_device(): pl.pallas_call(functools.partial(local_kernel, blocks, tokens), out_shape...]
  transfers between devices with their start and end apart: 1 -> 4, of which waited for: 0 -> 3; matrix products, arithmetic and copies ran while one was open for 61% -> 5% of each run, Pallas kernels for 0% -> 0%
where the time goes in v1:
time: 137 us
  blocking collectives  63.6 us (46%)
  waiting for transfers between devices  32.2 us (24%)
  Pallas kernels  20.1 us (15%)
  local copies, waits for them, and re-layouts  9.49 us (7%)
  starting transfers between devices  9.33 us (7%)
  other arithmetic  1.68 us (1%)
    all_gather x1, blocking collectives, gathered(): whole = lax.all_gather(packed, ('dp', 'ctx'), axis=0)  63.6 us
    ppermute x3, waiting for transfers between devices, per_device(): lax.ppermute(window, 'ctx', [(i, i + reach) for i in range(ctx - reach)])  32.1 us
    pallas_call x1, Pallas kernels, per_device(): pl.pallas_call(functools.partial(local_kernel, blocks, tokens), out_shape...  11.2 us
    pallas_call x1, Pallas kernels, per_device(): pl.pallas_call(functools.partial(final_kernel, blocks, tokens), out_shape...  8.85 us
    ppermute x3, starting transfers between devices, per_device(): lax.ppermute(window, 'ctx', [(i, i + reach) for i in range(ctx - reach)])  5.9 us
    transpose x2, local copies, waits for them, and re-layouts, per_device(): jnp.transpose(own[:, :, tokens - 2:], (0, 2, 1))  4.14 us
    ppermute x1, starting transfers between devices, per_device(): lax.ppermute(halo, 'ctx', [(i, i + 1) for i in range(ctx - 1)])  3.43 us
  transfers between devices with their start and end apart: 4, of which 3 were waited for; matrix products, arithmetic and copies ran while one was open for 5% of the time, Pallas kernels for 0%

profile of v1, /device:TPU:24, one launch (start us, length us, event | category | flops | bytes accessed | tf_op | source)
XLA Modules:
  0.0 136.5 jit_solution(15519945320405222696)
XLA Ops:
  0.0 2.8 %slice_bitcast_fusion = bf16[3,2,4096]{1,2,0:T(8,128)(2,1)S(1)} fusion(bf16[3,4096,128]{2,1,0:T(8,128)(2,1)} %bitcast.46), kind=kLoop, calls=%fused_computation | loop fusion | bytes 98304 | tf_op jit(solution)/shard_map/transpose | solution.py:152
  2.8 0.0 copy-start.1
  2.8 1.4 copy.8
  4.2 0.1 reshape.35
  4.3 3.4 %collective-permute-start = (bf16[3,64,128]{2,1,0:T(8,128)(2,1)S(1)}, bf16[3,64,128]{2,1,0:T(8,128)(2,1)S(1)}, u32[]{:S(2)}, u32[]{:S(2)}) collective-permute-start(bf16[3,64,128]{2,1,0:T(8,128)(2,1)S(1)} %reshape.35), channel_id=1, source_target_pairs={{0,1},{1,2},{2,3},{3,4},{4,5},{5,6},{6,7},{8,9},{9,10},{10,11},{11... | collective-permute-start | bytes 147464 | tf_op jit(solution)/shard_map/ppermute | solution.py:153
  7.7 0.1 pad_dynamic-slice_fusion.2
  7.8 0.1 fusion.6
  7.9 63.6 %all-gather.1 = f32[32,11,512]{2,1,0:T(8,128)S(1)} all-gather(f32[1,11,512]{2,1,0:T(8,128)S(1)} %maximum_bitcast_fusion), channel_id=2, replica_groups=mesh['dp'=4,'ctx'=8] {'dp','ctx'}, dimensions={0}, use_global_device_ids=true | all-gather | bytes 743424 | tf_op jit(solution)/shard_map/all_gather | solution.py:137
  71.5 1.3 copy.11
  72.8 2.0 %reshape.38 = f32[4,11,32,128]{3,2,1,0:T(8,128)} reshape(f32[4,11,8,512]{3,2,1,0:T(8,128)} %bitcast.54) | data formatting | bytes 1441792 | tf_op jit(solution)/shard_map/reshape | solution.py:140
  74.8 0.9 slice.30
  75.8 1.2 multiply_exponential_fusion
  77.1 0.9 slice.27.taps
  78.0 11.2 %shard_map.55 = (f32[4096,128]{1,0:T(8,128)S(1)}, f32[16,32,128]{2,1,0:T(8,128)S(1)}) custom-call(bf16[3,4096,128]{2,1,0:T(8,128)(2,1)S(1)} %bitcast.47, f32[3,64,128]{2,1,0:T(8,128)S(1)} %convert_element_type.3.halo, f32[3,3,32,128]{3,2,1,0:T(8,128)S(1)} %slice.27.taps, f32[32,128]{1,0:T(8,128)S(1)} %slice_bitcast_fusion.1.bias, ...), custom_call_target="tpu_custom_call" | custom-call | tf_op jit(solution)/shard_map/pallas_call | solution.py:160
  89.3 3.3 %collective-permute-start.1 = (f32[16,32,128]{2,1,0:T(8,128)S(1)}, f32[16,32,128]{2,1,0:T(8,128)S(1)}, u32[]{:S(2)}, u32[]{:S(2)}) collective-permute-start(f32[16,32,128]{2,1,0:T(8,128)S(1)} %get-tuple-element.7), channel_id=1, source_target_pairs={{0,1},{1,2},{2,3},{3,4},{4,5},{5,6},{6,7},{8,9},{9,10},{10,11},{11... | collective-permute-start | bytes 786440 | tf_op jit(solution)/shard_map/ppermute | solution.py:177
  92.6 8.0 %collective-permute-done.1 = f32[16,32,128]{2,1,0:T(8,128)S(1)} collective-permute-done((f32[16,32,128]{2,1,0:T(8,128)S(1)}, f32[16,32,128]{2,1,0:T(8,128)S(1)}, u32[]{:S(2)}, u32[]{:S(2)}) %collective-permute-start.1) | collective-permute-done | bytes 262176 | tf_op jit(solution)/shard_map/ppermute | solution.py:177
  100.5 0.1 fusion.1
  100.6 1.3 collective-permute-start.2
  101.9 9.5 %collective-permute-done.2 = f32[16,32,128]{2,1,0:T(8,128)S(1)} collective-permute-done((f32[16,32,128]{2,1,0:T(8,128)S(1)}, f32[16,32,128]{2,1,0:T(8,128)S(1)}, u32[]{:S(2)}, u32[]{:S(2)}) %collective-permute-start.2) | collective-permute-done | bytes 262176 | tf_op jit(solution)/shard_map/ppermute | solution.py:177
  111.4 0.1 fusion.3
  111.5 1.3 collective-permute-start.3
  112.8 14.7 %collective-permute-done.3 = f32[16,32,128]{2,1,0:T(8,128)S(1)} collective-permute-done((f32[16,32,128]{2,1,0:T(8,128)S(1)}, f32[16,32,128]{2,1,0:T(8,128)S(1)}, u32[]{:S(2)}, u32[]{:S(2)}) %collective-permute-start.3) | collective-permute-done | bytes 262176 | tf_op jit(solution)/shard_map/ppermute | solution.py:177
  127.5 0.1 fusion.carry
  127.7 8.8 %shard_map.56 = bf16[4096,128]{1,0:T(8,128)(2,1)} custom-call(bf16[3,4096,128]{2,1,0:T(8,128)(2,1)S(1)} %bitcast.48, f32[3,64,128]{2,1,0:T(8,128)S(1)} %convert_element_type.3.halo, f32[3,3,32,128]{3,2,1,0:T(8,128)S(1)} %slice.27.taps, f32[16,32,128]{2,1,0:T(8,128)S(1)} %bitcast.52, f32[16,32,128]{2,1,0:T(8,128)S(1)} %bitcast.50, ...), custom_call_target="tpu_custom_call" | custom-call | tf_op jit(solution)/shard_map/pallas_call | solution.py:181
  (15 shorter events, 0.1 us)
Async XLA Ops:
  2.8 4.9 %copy-start.1 = (f32[3,3,512]{2,1,0:T(4,128)S(1)}, f32[3,3,512]{2,1,0:T(4,128)}, u32[]{:S(2)}) copy-start(f32[3,3,512]{2,1,0:T(4,128)} %param.6) | copy-start | bytes 55300
  2.8 5.0 %copy-start.4 = (f32[512]{0:T(512)S(1)}, f32[512]{0:T(512)}, u32[]{:S(2)}) copy-start(f32[512]{0:T(512)} %param.9) | copy-start | bytes 6148
  2.8 5.1 %copy-start.2 = (f32[4,512]{1,0:T(4,128)S(1)}, f32[4,512]{1,0:T(4,128)}, u32[]{:S(2)}) copy-start(f32[4,512]{1,0:T(4,128)} %param.8) | copy-start | bytes 24580
  2.8 5.1 %copy-start.3 = (f32[4,512]{1,0:T(4,128)S(1)}, f32[4,512]{1,0:T(4,128)}, u32[]{:S(2)}) copy-start(f32[4,512]{1,0:T(4,128)} %param.7) | copy-start | bytes 24580
  4.3 73.7 %collective-permute-start = (bf16[3,64,128]{2,1,0:T(8,128)(2,1)S(1)}, bf16[3,64,128]{2,1,0:T(8,128)(2,1)S(1)}, u32[]{:S(2)}, u32[]{:S(2)}) collective-permute-start(bf16[3,64,128]{2,1,0:T(8,128)(2,1)S(1)} %reshape.35), channel_id=1, source_target_pairs={{0,1},{1,2},{2,3},{3,4},{4,5},{5,6},{6,7},{8,9},{9,10},{10,11},{11... | collective-permute-start | bytes 147464 | tf_op jit(solution)/shard_map/ppermute | solution.py:153
  71.5 6.5 %copy-start = (bf16[1,3,4096,128]{3,2,1,0:T(8,128)(2,1)S(1)}, bf16[1,3,4096,128]{3,2,1,0:T(8,128)(2,1)}, u32[]{:S(2)}) copy-start(bf16[1,3,4096,128]{3,2,1,0:T(8,128)(2,1)} %param.5) | copy-start | bytes 9437188
  89.3 11.3 %collective-permute-start.1 = (f32[16,32,128]{2,1,0:T(8,128)S(1)}, f32[16,32,128]{2,1,0:T(8,128)S(1)}, u32[]{:S(2)}, u32[]{:S(2)}) collective-permute-start(f32[16,32,128]{2,1,0:T(8,128)S(1)} %get-tuple-element.7), channel_id=1, source_target_pairs={{0,1},{1,2},{2,3},{3,4},{4,5},{5,6},{6,7},{8,9},{9,10},{10,11},{11... | collective-permute-start | bytes 786440 | tf_op jit(solution)/shard_map/ppermute | solution.py:177
  100.6 10.8 %collective-permute-start.2 = (f32[16,32,128]{2,1,0:T(8,128)S(1)}, f32[16,32,128]{2,1,0:T(8,128)S(1)}, u32[]{:S(2)}, u32[]{:S(2)}) collective-permute-start(f32[16,32,128]{2,1,0:T(8,128)S(1)} %fusion.1), channel_id=1, source_target_pairs={{0,2},{1,3},{2,4},{3,5},{4,6},{5,7},{8,10},{9,11},{10,12},{11,13},... | collective-permute-start | bytes 786440 | tf_op jit(solution)/shard_map/ppermute | solution.py:177
  111.5 16.0 %collective-permute-start.3 = (f32[16,32,128]{2,1,0:T(8,128)S(1)}, f32[16,32,128]{2,1,0:T(8,128)S(1)}, u32[]{:S(2)}, u32[]{:S(2)}) collective-permute-start(f32[16,32,128]{2,1,0:T(8,128)S(1)} %fusion.3), channel_id=1, source_target_pairs={{0,4},{1,5},{2,6},{3,7},{8,12},{9,13},{10,14},{11,15},{16,20},{17,... | collective-permute-start | bytes 786440 | tf_op jit(solution)/shard_map/ppermute | solution.py:177

commit v2 on v1

v2 whole, which is shorter than its diff:
```python
import functools
import jax
import jax.numpy as jnp
from jax import lax
from jax.experimental import pallas as pl
from jax.experimental.pallas import tpu as pltpu
from jax.sharding import PartitionSpec as P

ORDER = 16
LANES = 128
SUB = 8
GROUP = LANES * SUB


def identity(size):
    rows = lax.broadcasted_iota(jnp.int32, (size, size), 0)
    columns = lax.broadcasted_iota(jnp.int32, (size, size), 1)
    return (rows == columns).astype(jnp.bfloat16)


def flipped(eye, block):
    return lax.dot_general(
        eye, block, (((1,), (1,)), ((), ())), preferred_element_type=jnp.float32
    )


def to_tokens(eye, source, target, blocks, group, tokens):
    for sub in range(SUB):
        block = group * SUB + sub
        tile = source[pl.ds(pl.multiple_of(block * LANES, LANES), LANES), :]
        target[pl.ds(2 * blocks + block, tokens, stride=blocks), :] = flipped(eye, tile)


def rows_at(ref, token, blocks, group):
    return ref[pl.ds(pl.multiple_of(token * blocks + group * SUB, SUB), SUB), :]


def rounded(value):
    return value.astype(jnp.bfloat16).astype(jnp.float32)


def tree_sum(terms):
    terms = list(terms)
    while len(terms) > 1:
        terms = [a + b for a, b in zip(terms[::2], terms[1::2])]
    return terms[0]


MESH = pl.DeviceIdType.MESH


def mixer_kernel(dp, ctx, blocks, tokens, inside, rows, *refs):
    qkv, given, out = refs[:3]
    q_s, k_s, v_s, y_s, held, table, last, window, came, carry = refs[3:13]
    par_send, par_recv, dp_send, dp_recv, halo_send, halo_recv, step_send, step_recv = refs[13:]
    me = lax.axis_index("ctx")
    own_dp = lax.axis_index("dp")
    groups = blocks // SUB
    reaches = [1 << s for s in range((ctx - 1).bit_length())]
    modes = ORDER // dp
    height = 2 * modes + rows
    across = lax.rem(own_dp + dp // 2, dp)
    beside = own_dp + 1 - 2 * lax.rem(own_dp, 2)

    barrier = pltpu.get_barrier_semaphore()

    def greet(k, _):
        pl.semaphore_signal(
            barrier, inc=1, device_id={"ctx": lax.rem(me + k, ctx)}, device_id_type=MESH
        )
        return 0

    lax.fori_loop(1, ctx, greet, 0)
    greeted = ctx - 1
    if inside:
        for other in (across, beside):
            pl.semaphore_signal(barrier, inc=1, device_id={"dp": other}, device_id_type=MESH)
        greeted += 2
    pl.semaphore_wait(barrier, greeted)

    def remote(source, target, send, recv, where):
        return pltpu.make_async_remote_copy(
            src_ref=source,
            dst_ref=target,
            send_sem=send,
            recv_sem=recv,
            device_id=where,
            device_id_type=MESH,
        )

    def share(k):
        to = {"ctx": lax.rem(me + k, ctx)}
        return remote(given, held.at[own_dp, me], par_send.at[k], par_recv.at[k], to)

    def start_share(k, _):
        share(k).start()
        return 0

    def wait_share(k, _):
        share(k).wait()
        return 0

    if inside:
        lax.fori_loop(1, ctx, start_share, 0)
        held[own_dp, me] = given[...]

    eye = identity(tokens)

    def turn(group, _):
        to_tokens(eye, qkv.at[0], q_s, blocks, group, tokens)
        to_tokens(eye, qkv.at[1], k_s, blocks, group, tokens)
        to_tokens(eye, qkv.at[2], v_s, blocks, group, tokens)
        return 0

    lax.fori_loop(0, groups, turn, 0)

    streams = (q_s, k_s, v_s)
    ends = [
        remote(
            ref.at[pl.ds(tokens * blocks, 2 * blocks), :],
            ref.at[pl.ds(0, 2 * blocks), :],
            halo_send.at[w],
            halo_recv.at[w],
            {"ctx": lax.rem(me + 1, ctx)},
        )
        for w, ref in enumerate(streams)
    ]

    @pl.when(me + 1 < ctx)
    def _():
        for copy in ends:
            copy.start()

    @pl.when(me == 0)
    def _():
        for ref in streams:
            ref[0 : 2 * blocks, :] = jnp.zeros((2 * blocks, LANES), jnp.float32)

    for s, reach in enumerate(reaches):

        @pl.when(me < reach)
        def _(s=s):
            came[s] = jnp.zeros_like(came[s])

    if inside:
        lax.fori_loop(1, ctx, wait_share, 0)
        part = held.at[own_dp]
        far = remote(part, part, dp_send.at[0], dp_recv.at[0], {"dp": across})
        near = remote(part, part, dp_send.at[1], dp_recv.at[1], {"dp": beside})
        far.start()
        near.start()
        far.wait()
        other = held.at[across]
        last_part = remote(other, other, dp_send.at[2], dp_recv.at[2], {"dp": beside})
        last_part.start()
        near.wait()
        last_part.wait()
        each = blocks // ctx

        def place(d, _):
            for c in range(ctx):
                for h in range(height):
                    table[d * height + h, each * c : each * (c + 1), :] = held[
                        d, c, each * h : each * (h + 1), :
                    ]
            return 0

        lax.fori_loop(0, dp, place, 0)
        source = table
    else:
        source = given

    @pl.when(me > 0)
    def _():
        for copy in ends:
            copy.wait_recv()

    def owned(group):
        return pl.ds(group * SUB, SUB)

    def rate_of(n, group):
        return source[(n // modes) * height + n % modes, owned(group), :]

    def coef_of(n, group):
        residue = source[(n // modes) * height + modes + n % modes, owned(group), :]
        return residue * jnp.sqrt(2.0 * rate_of(n, group) / ORDER)

    def extra(e, group):
        return source[(e // rows) * height + 2 * modes + e % rows, owned(group), :]

    def step_copy(s, group):
        ref = last.at[group] if s == 0 else window.at[s - 1, group]
        return remote(
            ref,
            came.at[s, group],
            step_send.at[s, group],
            step_recv.at[s, group],
            {"ctx": lax.rem(me + reaches[s], ctx)},
        )

    def send(s, group):
        @pl.when(me + reaches[s] < ctx)
        def _():
            step_copy(s, group).start()

    def scan(group):
        tap = [[extra(3 * i + w, group) for i in range(3)] for w in (1, 2)]
        direct = extra(9, group)
        dec = [jnp.exp(-rate_of(n, group)) for n in range(ORDER)]
        coe = [coef_of(n, group) for n in range(ORDER)]

        def step(t, state):
            k2, k1, v2, v1, states = state
            k0 = rows_at(k_s, t + 2, blocks, group)
            v0 = rows_at(v_s, t + 2, blocks, group)
            fk = tap[0][0] * k0 + tap[0][1] * k1 + tap[0][2] * k2
            fv = tap[1][0] * v0 + tap[1][1] * v1 + tap[1][2] * v2
            u = rounded(fk * fv)
            states = tuple(d * s + u for d, s in zip(dec, states))
            y = tree_sum(c * s for c, s in zip(coe, states)) + direct * u
            y_s[pl.ds(pl.multiple_of(t * blocks + group * SUB, SUB), SUB), :] = y
            return (k1, k0, v1, v0, states)

        zero = jnp.zeros((SUB, LANES), jnp.float32)
        start = (
            rows_at(k_s, 0, blocks, group),
            rows_at(k_s, 1, blocks, group),
            rows_at(v_s, 0, blocks, group),
            rows_at(v_s, 1, blocks, group),
            (zero,) * ORDER,
        )
        states = lax.fori_loop(0, tokens, step, start, unroll=4)[4]
        for n in range(ORDER):
            last[group, n] = states[n]
        send(0, group)

    def combine(s, group):
        @pl.when(me >= reaches[s])
        def _():
            step_copy(s, group).wait_recv()

        for n in range(ORDER):
            rate = rate_of(n, group)
            total = came[s, group, n]
            if s > 0:
                past = jnp.exp(-rate * (tokens * (reaches[s] - 1.0)))
                total = carry[group, n] + past * total
            carry[group, n] = total
            if s + 1 < len(reaches):
                window[s, group, n] = last[group, n] + jnp.exp(-rate * tokens) * total
        if s + 1 < len(reaches):
            send(s + 1, group)

    def finish(group):
        tap = [extra(3 * i, group) for i in range(3)]
        dec = [jnp.exp(-rate_of(n, group)) for n in range(ORDER)]
        first = tuple(coef_of(n, group) * carry[group, n] for n in range(ORDER))

        def step(t, state):
            q2, q1, parts = state
            q0 = rows_at(q_s, t + 2, blocks, group)
            parts = tuple(d * z for d, z in zip(dec, parts))
            long = rounded(rows_at(y_s, t, blocks, group) + tree_sum(parts))
            fq = tap[0] * q0 + tap[1] * q1 + tap[2] * q2
            y_s[pl.ds(pl.multiple_of(t * blocks + group * SUB, SUB), SUB), :] = fq * long
            return (q1, q0, parts)

        start = (rows_at(q_s, 0, blocks, group), rows_at(q_s, 1, blocks, group), first)
        lax.fori_loop(0, tokens, step, start, unroll=4)
        for sub in range(SUB):
            block = group * SUB + sub
            tile = y_s[pl.ds(block, tokens, stride=blocks), :].astype(jnp.bfloat16)
            out[block * LANES : (block + 1) * LANES, :] = flipped(eye, tile).astype(jnp.bfloat16)

    for group in range(groups):
        scan(group)
        if group > 0:
            combine(0, group - 1)
    combine(0, groups - 1)
    for s in range(1, len(reaches) - 1):
        for group in range(groups):
            combine(s, group)
    for group in range(groups):
        if len(reaches) > 1:
            combine(len(reaches) - 1, group)
        finish(group)

    @pl.when(me + 1 < ctx)
    def _():
        for copy in ends:
            copy.wait_send()

    for s, reach in enumerate(reaches):

        @pl.when(me + reach < ctx)
        def _(s=s):
            for group in range(groups):
                step_copy(s, group).wait_send()


def local_pack(taps, rate_table, residue_table, bias, dp):
    width = bias.shape[0]
    rows = -(-10 // dp)
    extra = jnp.concatenate(
        [taps.reshape(9, width), bias[None], jnp.zeros((rows * dp - 10, width), jnp.float32)]
    )
    own = lax.dynamic_slice_in_dim(extra, lax.axis_index("dp") * rows, rows, 0)
    return jnp.concatenate([rate_table, residue_table, own])


def gathered(packed, dp, ctx):
    height, width = packed.shape
    whole = lax.all_gather(packed, ("dp", "ctx"), axis=0)
    whole = whole.reshape(dp, ctx, height, width).transpose(0, 2, 1, 3)
    return whole.reshape(dp * height, ctx * width // LANES, LANES)


def per_device(dp, ctx, qkv, taps, rate_table, residue_table, bias):
    _, _, chans, tokens = qkv.shape
    blocks = chans // LANES
    modes, width = rate_table.shape
    rows = -(-10 // dp)
    height = 2 * modes + rows
    inside = dp == 4 and width % LANES == 0
    packed = local_pack(taps, rate_table, residue_table, bias, dp)
    if inside:
        given = packed.reshape(height * width // LANES, LANES)
    else:
        given = gathered(packed, dp, ctx)
    groups = blocks // SUB
    steps = (ctx - 1).bit_length()
    wide = (tokens + 2) * blocks
    each = height * max(width // LANES, 1) if inside else 8
    vmem = pl.BlockSpec(memory_space=pltpu.VMEM)
    slab = (groups, ORDER, SUB, LANES)
    f32 = jnp.float32
    out = pl.pallas_call(
        functools.partial(mixer_kernel, dp, ctx, blocks, tokens, inside, rows),
        out_shape=jax.ShapeDtypeStruct((chans, tokens), jnp.bfloat16),
        in_specs=[vmem] * 2,
        out_specs=vmem,
        scratch_shapes=[
            pltpu.VMEM((wide, LANES), f32),
            pltpu.VMEM((wide, LANES), f32),
            pltpu.VMEM((wide, LANES), f32),
            pltpu.VMEM((tokens * blocks, LANES), f32),
            pltpu.VMEM((dp, ctx, each, LANES) if inside else (1, 1, each, LANES), f32),
            pltpu.VMEM((dp * height, blocks, LANES) if inside else (1, SUB, LANES), f32),
            pltpu.VMEM(slab, f32),
            pltpu.VMEM((max(steps - 1, 1),) + slab, f32),
            pltpu.VMEM((steps,) + slab, f32),
            pltpu.VMEM(slab, f32),
            pltpu.SemaphoreType.DMA((ctx,)),
            pltpu.SemaphoreType.DMA((ctx,)),
            pltpu.SemaphoreType.DMA((3,)),
            pltpu.SemaphoreType.DMA((3,)),
            pltpu.SemaphoreType.DMA((3,)),
            pltpu.SemaphoreType.DMA((3,)),
            pltpu.SemaphoreType.DMA((steps, groups)),
            pltpu.SemaphoreType.DMA((steps, groups)),
        ],
        compiler_params=pltpu.CompilerParams(
            collective_id=0, has_side_effects=True, vmem_limit_bytes=48 * 1024 * 1024
        ),
    )(qkv[0], given)
    return out[None]


def solution(mesh):
    in_specs = (
        P("dp", None, None, "ctx"),
        P(None, None, "ctx"),
        P("dp", "ctx"),
        P("dp", "ctx"),
        P("ctx"),
    )
    return jax.shard_map(
        functools.partial(per_device, mesh.shape["dp"], mesh.shape["ctx"]),
        mesh=mesh,
        in_specs=in_specs,
        out_specs=P("dp", None, "ctx"),
        check_vma=False,
    )
```

time: 137 us -> 51.2 us (0.37)
  blocking collectives: 63.6 us -> 0 us
  waiting for transfers between devices: 32.2 us -> 0 us
  Pallas kernels: 20.1 us -> 45.4 us
  starting transfers between devices: 9.33 us -> 0 us
  local copies, waits for them, and re-layouts: 9.49 us -> 3.69 us
    all_gather x1 -> x0, blocking collectives: 63.6 us -> none  [gathered(): whole = lax.all_gather(packed, ('dp', 'ctx'), axis=0)]
    ppermute x4 -> x0, waiting for transfers between devices: 32.2 us -> none  [the longest x3 32.1 us: per_device(): lax.ppermute(window, 'ctx', [(i, i + reach) for i in range(ctx - reach)])]
    pallas_call x2 -> x1, Pallas kernels: 20.1 us -> 45.4 us  [per_device(): pl.pallas_call(functools.partial(mixer_kernel, dp, ctx, blocks, tokens, i...]
    ppermute x4 -> x0, starting transfers between devices: 9.33 us -> none  [the longest x3 5.9 us: per_device(): lax.ppermute(window, 'ctx', [(i, i + reach) for i in range(ctx - reach)])]
    transpose x2 -> x0, local copies, waits for them, and re-layouts: 4.14 us -> none  [per_device(): jnp.transpose(own[:, :, tokens - 2:], (0, 2, 1))]
    unnamed x10 -> x3, local copies, waits for them, and re-layouts: 0.03 us -> 2.86 us
    reshape x4 -> x2, local copies, waits for them, and re-layouts: 3.37 us -> 0.75 us  [the longest x1 0.75 us: local_pack(): taps.reshape(9, width)]
    slice x2 -> x0, local copies, waits for them, and re-layouts: 1.87 us -> none  [the longest x1 0.94 us: gathered(): rest = whole[:, 2 * modes:].reshape(dp * rows, blocks, LANES)]
  transfers between devices with their start and end apart: 4 -> 0, of which waited for: 3 -> 0; matrix products, arithmetic and copies ran while one was open for 5% -> 0% of each run, Pallas kernels for 0% -> 0%
where the time goes in v2:
time: 51.2 us; the launch traced here: 50.6 us
  Pallas kernels  45.4 us (89%)
  local copies, waits for them, and re-layouts  3.69 us (7%)
  other arithmetic  1.49 us (3%)
    pallas_call x1, Pallas kernels, per_device(): pl.pallas_call(functools.partial(mixer_kernel, dp, ctx, blocks, tokens, i...  45.4 us
    unnamed x3, local copies, waits for them, and re-layouts  2.86 us

profile of v2, /device:TPU:24, one launch (start us, length us, event | category | flops | bytes accessed | tf_op | source)
XLA Modules:
  0.0 50.6 jit_solution(16558672780520006145)
XLA Ops:
  0.0 0.1 pad_dynamic-slice_fusion.2
  0.1 0.8 %reshape.6 = f32[9,512]{1,0:T(8,128)S(1)} reshape(f32[3,3,512]{2,1,0:T(4,128)} %param.6) | data formatting | bytes 36864 | tf_op jit(solution)/shard_map/reshape | solution.py:305
  0.8 0.8 %fusion.1 = f32[3,512]{1,0:T(4,128)S(1)} fusion(s32[]{:T(128)S(6)} %select_n.3, f32[9,512]{1,0:T(8,128)S(1)} %reshape.6, f32[1,512]{1,0:T(1,128)} %bitcast.5, f32[3]{0:T(128)S(1)} %pad_dynamic-slice_fusion.2), kind=kLoop, calls=%fused_computation.4 | loop fusion | flops 3072 | bytes 26640 | tf_op jit(solution)/shard_map/concatenate | solution.py:304
  1.6 0.7 %pad_maximum_fusion = f32[11,512]{1,0:T(8,128)S(1)} fusion(f32[3,512]{1,0:T(4,128)S(1)} %fusion.1, f32[4,512]{1,0:T(4,128)} %param.8, f32[4,512]{1,0:T(4,128)} %param.7), kind=kLoop, calls=%fused_computation.2 | loop fusion | flops 11264 | bytes 45056 | tf_op jit(solution)/shard_map/concatenate | solution.py:308
  2.3 0.0 copy-start
  2.3 1.9 %copy-done = bf16[1,3,4096,128]{3,2,1,0:T(8,128)(2,1)S(1)} copy-done((bf16[1,3,4096,128]{3,2,1,0:T(8,128)(2,1)S(1)}, bf16[1,3,4096,128]{3,2,1,0:T(8,128)(2,1)}, u32[]{:S(2)}) %copy-start) | copy-done | bytes 3145752
  4.2 45.4 %shard_map.55 = bf16[4096,128]{1,0:T(8,128)(2,1)S(1)} custom-call(bf16[3,4096,128]{2,1,0:T(8,128)(2,1)S(1)} %bitcast.4, f32[44,128]{1,0:T(8,128)S(1)} %reshape.7.refs_1_), custom_call_target="tpu_custom_call" | custom-call | tf_op jit(solution)/shard_map/pallas_call | solution.py:337
  49.6 1.0 %copy.7 = bf16[1,4096,128]{2,1,0:T(8,128)(2,1)} copy(bf16[1,4096,128]{2,1,0:T(8,128)(2,1)S(1)} %bitcast.3) | data formatting | bytes 2097152
  (2 shorter events, 0.0 us)
Async XLA Ops:
  2.3 1.9 %copy-start = (bf16[1,3,4096,128]{3,2,1,0:T(8,128)(2,1)S(1)}, bf16[1,3,4096,128]{3,2,1,0:T(8,128)(2,1)}, u32[]{:S(2)}) copy-start(bf16[1,3,4096,128]{3,2,1,0:T(8,128)(2,1)} %param.5) | copy-start | bytes 9437188

commit v3 on v2

--- a/solution.py
+++ b/solution.py
@@ -27,7 +27,7 @@
 def to_tokens(eye, source, target, blocks, group, tokens):
     for sub in range(SUB):
         block = group * SUB + sub
-        tile = source[pl.ds(pl.multiple_of(block * LANES, LANES), LANES), :]
+        tile = source[pl.ds(block * LANES, LANES), :]
         target[pl.ds(2 * blocks + block, tokens, stride=blocks), :] = flipped(eye, tile)
 
 
@@ -51,16 +51,25 @@
 
 def mixer_kernel(dp, ctx, blocks, tokens, inside, rows, *refs):
     qkv, given, out = refs[:3]
-    q_s, k_s, v_s, y_s, held, table, last, window, came, carry = refs[3:13]
-    par_send, par_recv, dp_send, dp_recv, halo_send, halo_recv, step_send, step_recv = refs[13:]
+    raw, q_s, k_s, v_s, y_s, held, table, last, window, came, carry, load = refs[3:15]
+    par_send, par_recv, dp_send, dp_recv, halo_send, halo_recv, step_send, step_recv = refs[15:]
     me = lax.axis_index("ctx")
     own_dp = lax.axis_index("dp")
     groups = blocks // SUB
-    reaches = [1 << s for s in range((ctx - 1).bit_length())]
+    steps = (ctx - 1).bit_length()
+    pair = lax.div(me, 2)
+    second = lax.rem(me, 2)
     modes = ORDER // dp
     height = 2 * modes + rows
     across = lax.rem(own_dp + dp // 2, dp)
     beside = own_dp + 1 - 2 * lax.rem(own_dp, 2)
+
+    def fetch(group):
+        own = pl.ds(group * GROUP, GROUP)
+        return pltpu.make_async_copy(qkv.at[:, own, :], raw.at[:, own, :], load.at[group])
+
+    for group in range(groups):
+        fetch(group).start()
 
     barrier = pltpu.get_barrier_semaphore()
 
@@ -96,23 +105,52 @@
         share(k).start()
         return 0
 
-    def wait_share(k, _):
-        share(k).wait()
+    def relay(hop, k):
+        from_dp = across if hop == 2 else own_dp
+        block = held.at[from_dp, lax.rem(me + ctx - k, ctx)]
+        to = across if hop == 0 else beside
+        return remote(block, block, dp_send.at[hop, k], dp_recv.at[hop, k], {"dp": to})
+
+    def pass_on(k, _):
+        if not isinstance(k, int):
+            share(k).wait_recv()
+        relay(0, k).start()
+        relay(1, k).start()
+        return 0
+
+    def pass_far(k, _):
+        relay(0, k).wait_recv()
+        relay(2, k).start()
+        return 0
+
+    def arrive(k, _):
+        relay(1, k).wait_recv()
+        relay(2, k).wait_recv()
+        return 0
+
+    def all_sent(k, _):
+        for hop in range(3):
+            relay(hop, k).wait_send()
+        return 0
+
+    def share_sent(k, _):
+        share(k).wait_send()
         return 0
 
     if inside:
         lax.fori_loop(1, ctx, start_share, 0)
         held[own_dp, me] = given[...]
+        pass_on(0, 0)
 
     eye = identity(tokens)
 
-    def turn(group, _):
-        to_tokens(eye, qkv.at[0], q_s, blocks, group, tokens)
-        to_tokens(eye, qkv.at[1], k_s, blocks, group, tokens)
-        to_tokens(eye, qkv.at[2], v_s, blocks, group, tokens)
-        return 0
-
-    lax.fori_loop(0, groups, turn, 0)
+    for group in range(groups):
+        fetch(group).wait()
+        to_tokens(eye, raw.at[1], k_s, blocks, group, tokens)
+        to_tokens(eye, raw.at[2], v_s, blocks, group, tokens)
+        to_tokens(eye, raw.at[0], q_s, blocks, group, tokens)
+        if inside and group == groups // 2 - 1:
+            lax.fori_loop(1, ctx, pass_on, 0)
 
     streams = (q_s, k_s, v_s)
     ends = [
@@ -136,25 +174,21 @@
         for ref in streams:
             ref[0 : 2 * blocks, :] = jnp.zeros((2 * blocks, LANES), jnp.float32)
 
-    for s, reach in enumerate(reaches):
-
-        @pl.when(me < reach)
+    def sends(s):
+        return lax.rem(pair, 1 << s) == (1 << (s - 1)) - 1
+
+    def takes(s):
+        return lax.rem(pair, 1 << s) >= 1 << (s - 1)
+
+    for s in range(1, steps):
+
+        @pl.when(jnp.logical_not(takes(s)))
         def _(s=s):
             came[s] = jnp.zeros_like(came[s])
 
     if inside:
-        lax.fori_loop(1, ctx, wait_share, 0)
-        part = held.at[own_dp]
-        far = remote(part, part, dp_send.at[0], dp_recv.at[0], {"dp": across})
-        near = remote(part, part, dp_send.at[1], dp_recv.at[1], {"dp": beside})
-        far.start()
-        near.start()
-        far.wait()
-        other = held.at[across]
-        last_part = remote(other, other, dp_send.at[2], dp_recv.at[2], {"dp": beside})
-        last_part.start()
-        near.wait()
-        last_part.wait()
+        lax.fori_loop(0, ctx, pass_far, 0)
+        lax.fori_loop(0, ctx, arrive, 0)
         each = blocks // ctx
 
         def place(d, _):
@@ -188,20 +222,23 @@
     def extra(e, group):
         return source[(e // rows) * height + 2 * modes + e % rows, owned(group), :]
 
-    def step_copy(s, group):
-        ref = last.at[group] if s == 0 else window.at[s - 1, group]
+    def swap(group):
         return remote(
-            ref,
+            last.at[group],
+            came.at[0, group],
+            step_send.at[0, group],
+            step_recv.at[0, group],
+            {"ctx": me + 1 - 2 * second},
+        )
+
+    def spread(s, j, group):
+        return remote(
+            window.at[s - 1, group],
             came.at[s, group],
-            step_send.at[s, group],
+            step_send.at[(1 << (s - 1)) + j, group],
             step_recv.at[s, group],
-            {"ctx": lax.rem(me + reaches[s], ctx)},
-        )
-
-    def send(s, group):
-        @pl.when(me + reaches[s] < ctx)
-        def _():
-            step_copy(s, group).start()
+            {"ctx": lax.rem(me + 2 * (j + 1), ctx)},
+        )
 
     def scan(group):
         tap = [[extra(3 * i + w, group) for i in range(3)] for w in (1, 2)]
@@ -232,24 +269,43 @@
         states = lax.fori_loop(0, tokens, step, start, unroll=4)[4]
         for n in range(ORDER):
             last[group, n] = states[n]
-        send(0, group)
+        swap(group).start()
 
     def combine(s, group):
-        @pl.when(me >= reaches[s])
-        def _():
-            step_copy(s, group).wait_recv()
-
+        if s == 0:
+            swap(group).wait_recv()
+        else:
+
+            @pl.when(takes(s))
+            def _():
+                spread(s, 0, group).wait_recv()
+
+            ahead = jnp.maximum(lax.rem(pair, 1 << s) - (1 << (s - 1)), 0)
+            ahead = ahead.astype(jnp.float32) * (2.0 * tokens)
         for n in range(ORDER):
             rate = rate_of(n, group)
-            total = came[s, group, n]
-            if s > 0:
-                past = jnp.exp(-rate * (tokens * (reaches[s] - 1.0)))
-                total = carry[group, n] + past * total
-            carry[group, n] = total
-            if s + 1 < len(reaches):
-                window[s, group, n] = last[group, n] + jnp.exp(-rate * tokens) * total
-        if s + 1 < len(reaches):
-            send(s + 1, group)
+            if s == 0:
+                mine, other = last[group, n], came[0, group, n]
+                first = jnp.where(second == 0, mine, other)
+                later = jnp.where(second == 0, other, mine)
+                window[0, group, n] = later + jnp.exp(-rate * tokens) * first
+            else:
+                total = jnp.exp(-rate * ahead) * came[s, group, n]
+                if s > 1:
+                    total = total + carry[group, n]
+                if s + 1 < steps:
+                    within = jnp.exp(-rate * (2.0 * tokens)) * total
+                    window[s, group, n] = window[0, group, n] + within
+                    carry[group, n] = total
+                else:
+                    behind = came[0, group, n] + jnp.exp(-rate * tokens) * total
+                    carry[group, n] = jnp.where(second == 0, total, behind)
+        if s + 1 < steps:
+
+            @pl.when(sends(s + 1))
+            def _():
+                for j in range(1 << s):
+                    spread(s + 1, j, group).start()
 
     def finish(group):
         tap = [extra(3 * i, group) for i in range(3)]
@@ -274,15 +330,15 @@
 
     for group in range(groups):
         scan(group)
-        if group > 0:
-            combine(0, group - 1)
-    combine(0, groups - 1)
-    for s in range(1, len(reaches) - 1):
-        for group in range(groups):
-            combine(s, group)
+        for s in range(steps - 1):
+            if group > s:
+                combine(s, group - 1 - s)
+    for late in range(groups, groups + steps - 1):
+        for s in range(steps - 1):
+            if 0 <= late - 1 - s < groups:
+                combine(s, late - 1 - s)
     for group in range(groups):
-        if len(reaches) > 1:
-            combine(len(reaches) - 1, group)
+        combine(steps - 1, group)
         finish(group)
 
     @pl.when(me + 1 < ctx)
@@ -290,12 +346,18 @@
         for copy in ends:
             copy.wait_send()
 
-    for s, reach in enumerate(reaches):
-
-        @pl.when(me + reach < ctx)
+    if inside:
+        lax.fori_loop(1, ctx, share_sent, 0)
+        lax.fori_loop(0, ctx, all_sent, 0)
+    for group in range(groups):
+        swap(group).wait_send()
+    for s in range(1, steps):
+
+        @pl.when(sends(s))
         def _(s=s):
-            for group in range(groups):
-                step_copy(s, group).wait_send()
+            for j in range(1 << (s - 1)):
+                for group in range(groups):
+                    spread(s, j, group).wait_send()
 
 
 def local_pack(taps, rate_table, residue_table, bias, dp):
@@ -337,9 +399,10 @@
     out = pl.pallas_call(
         functools.partial(mixer_kernel, dp, ctx, blocks, tokens, inside, rows),
         out_shape=jax.ShapeDtypeStruct((chans, tokens), jnp.bfloat16),
-        in_specs=[vmem] * 2,
+        in_specs=[pl.BlockSpec(memory_space=pl.ANY), vmem],
         out_specs=vmem,
         scratch_shapes=[
+            pltpu.VMEM((3, chans, tokens), jnp.bfloat16),
             pltpu.VMEM((wide, LANES), f32),
             pltpu.VMEM((wide, LANES), f32),
             pltpu.VMEM((wide, LANES), f32),
@@ -350,13 +413,14 @@
             pltpu.VMEM((max(steps - 1, 1),) + slab, f32),
             pltpu.VMEM((steps,) + slab, f32),
             pltpu.VMEM(slab, f32),
+            pltpu.SemaphoreType.DMA((groups,)),
             pltpu.SemaphoreType.DMA((ctx,)),
             pltpu.SemaphoreType.DMA((ctx,)),
+            pltpu.SemaphoreType.DMA((3, ctx if inside else 1)),
+            pltpu.SemaphoreType.DMA((3, ctx if inside else 1)),
             pltpu.SemaphoreType.DMA((3,)),
             pltpu.SemaphoreType.DMA((3,)),
-            pltpu.SemaphoreType.DMA((3,)),
-            pltpu.SemaphoreType.DMA((3,)),
-            pltpu.SemaphoreType.DMA((steps, groups)),
+            pltpu.SemaphoreType.DMA((ctx // 2, groups)),
             pltpu.SemaphoreType.DMA((steps, groups)),
         ],
         compiler_params=pltpu.CompilerParams(

time: 51.2 us -> 43.8 us (0.86)
  Pallas kernels: 45.4 us -> 38.3 us
    pallas_call x1, Pallas kernels: 45.4 us -> 38.3 us  [per_device(): pl.pallas_call(functools.partial(mixer_kernel, dp, ctx, blocks, tokens, i...]
where the time goes in v3:
time: 43.8 us; the launch traced here: 43.5 us
  Pallas kernels  38.3 us (87%)
  local copies, waits for them, and re-layouts  3.69 us (8%)
  other arithmetic  1.49 us (3%)
    pallas_call x1, Pallas kernels, per_device(): pl.pallas_call(functools.partial(mixer_kernel, dp, ctx, blocks, tokens, i...  38.3 us
    unnamed x3, local copies, waits for them, and re-layouts  2.86 us

profile of v3, /device:TPU:24, one launch (start us, length us, event | category | flops | bytes accessed | tf_op | source)
XLA Modules:
  0.0 43.5 jit_solution(8794033328217771574)
XLA Ops:
  0.0 0.1 pad_dynamic-slice_fusion.2
  0.1 0.8 %reshape.6 = f32[9,512]{1,0:T(8,128)S(1)} reshape(f32[3,3,512]{2,1,0:T(4,128)} %param.6) | data formatting | bytes 36864 | tf_op jit(solution)/shard_map/reshape | solution.py:367
  0.8 0.8 %fusion.1 = f32[3,512]{1,0:T(4,128)S(1)} fusion(s32[]{:T(128)S(6)} %select_n.3, f32[9,512]{1,0:T(8,128)S(1)} %reshape.6, f32[1,512]{1,0:T(1,128)} %bitcast.5, f32[3]{0:T(128)S(1)} %pad_dynamic-slice_fusion.2), kind=kLoop, calls=%fused_computation.4 | loop fusion | flops 3072 | bytes 26640 | tf_op jit(solution)/shard_map/concatenate | solution.py:366
  1.6 0.7 %pad_maximum_fusion = f32[11,512]{1,0:T(8,128)S(1)} fusion(f32[3,512]{1,0:T(4,128)S(1)} %fusion.1, f32[4,512]{1,0:T(4,128)} %param.8, f32[4,512]{1,0:T(4,128)} %param.7), kind=kLoop, calls=%fused_computation.2 | loop fusion | flops 11264 | bytes 45056 | tf_op jit(solution)/shard_map/concatenate | solution.py:370
  2.3 0.0 copy-start
  2.3 1.9 %copy-done = bf16[1,3,4096,128]{3,2,1,0:T(8,128)(2,1)S(1)} copy-done((bf16[1,3,4096,128]{3,2,1,0:T(8,128)(2,1)S(1)}, bf16[1,3,4096,128]{3,2,1,0:T(8,128)(2,1)}, u32[]{:S(2)}) %copy-start) | copy-done | bytes 3145752
  4.2 38.3 %shard_map.55 = bf16[4096,128]{1,0:T(8,128)(2,1)S(1)} custom-call(bf16[3,4096,128]{2,1,0:T(8,128)(2,1)S(1)} %bitcast.4, f32[44,128]{1,0:T(8,128)S(1)} %reshape.7.refs_1_), custom_call_target="tpu_custom_call" | custom-call | tf_op jit(solution)/shard_map/pallas_call | solution.py:399
  42.5 1.0 %copy.7 = bf16[1,4096,128]{2,1,0:T(8,128)(2,1)} copy(bf16[1,4096,128]{2,1,0:T(8,128)(2,1)S(1)} %bitcast.3) | data formatting | bytes 2097152
  (2 shorter events, 0.0 us)
Async XLA Ops:
  2.3 1.9 %copy-start = (bf16[1,3,4096,128]{3,2,1,0:T(8,128)(2,1)S(1)}, bf16[1,3,4096,128]{3,2,1,0:T(8,128)(2,1)}, u32[]{:S(2)}) copy-start(bf16[1,3,4096,128]{3,2,1,0:T(8,128)(2,1)} %param.5) | copy-start | bytes 9437188

commit v4 on v3

--- a/solution.py
+++ b/solution.py
@@ -50,7 +50,10 @@
 
 
 def mixer_kernel(dp, ctx, blocks, tokens, inside, rows, *refs):
-    qkv, given, out = refs[:3]
+    tables = 4 if inside else 1
+    qkv, given = refs[0], refs[1 : 1 + tables]
+    refs = refs[tables - 1 :]
+    out = refs[2]
     raw, q_s, k_s, v_s, y_s, held, table, last, window, came, carry, load = refs[3:15]
     par_send, par_recv, dp_send, dp_recv, halo_send, halo_recv, step_send, step_recv = refs[15:]
     me = lax.axis_index("ctx")
@@ -71,6 +74,26 @@
     for group in range(groups):
         fetch(group).start()
 
+    if inside:
+        rate_in, residue_in, taps_in, bias_in = given
+        each = blocks // ctx
+        for b in range(each):
+            lanes = slice(LANES * b, LANES * (b + 1))
+            for h in range(modes):
+                at = each * h + b
+                held[own_dp, me, at : at + 1, :] = rate_in[h : h + 1, lanes]
+                at += each * modes
+                held[own_dp, me, at : at + 1, :] = residue_in[h : h + 1, lanes]
+            for r in range(rows):
+                line = bias_in[:, lanes]
+                for d in range(dp):
+                    e = d * rows + r
+                    if e < 9:
+                        tap = taps_in[e // 3, e % 3 : e % 3 + 1, lanes]
+                        line = jnp.where(own_dp == d, tap, line)
+                at = each * (2 * modes + r) + b
+                held[own_dp, me, at : at + 1, :] = line
+
     barrier = pltpu.get_barrier_semaphore()
 
     def greet(k, _):
@@ -99,7 +122,8 @@
 
     def share(k):
         to = {"ctx": lax.rem(me + k, ctx)}
-        return remote(given, held.at[own_dp, me], par_send.at[k], par_recv.at[k], to)
+        block = held.at[own_dp, me]
+        return remote(block, block, par_send.at[k], par_recv.at[k], to)
 
     def start_share(k, _):
         share(k).start()
@@ -139,7 +163,6 @@
 
     if inside:
         lax.fori_loop(1, ctx, start_share, 0)
-        held[own_dp, me] = given[...]
         pass_on(0, 0)
 
     eye = identity(tokens)
@@ -189,7 +212,6 @@
     if inside:
         lax.fori_loop(0, ctx, pass_far, 0)
         lax.fori_loop(0, ctx, arrive, 0)
-        each = blocks // ctx
 
         def place(d, _):
             for c in range(ctx):
@@ -202,7 +224,7 @@
         lax.fori_loop(0, dp, place, 0)
         source = table
     else:
-        source = given
+        source = given[0]
 
     @pl.when(me > 0)
     def _():
@@ -384,11 +406,10 @@
     rows = -(-10 // dp)
     height = 2 * modes + rows
     inside = dp == 4 and width % LANES == 0
-    packed = local_pack(taps, rate_table, residue_table, bias, dp)
-    if inside:
-        given = packed.reshape(height * width // LANES, LANES)
+    if inside:
+        given = (rate_table, residue_table, taps, bias[None])
     else:
-        given = gathered(packed, dp, ctx)
+        given = (gathered(local_pack(taps, rate_table, residue_table, bias, dp), dp, ctx),)
     groups = blocks // SUB
     steps = (ctx - 1).bit_length()
     wide = (tokens + 2) * blocks
@@ -399,7 +420,7 @@
     out = pl.pallas_call(
         functools.partial(mixer_kernel, dp, ctx, blocks, tokens, inside, rows),
         out_shape=jax.ShapeDtypeStruct((chans, tokens), jnp.bfloat16),
-        in_specs=[pl.BlockSpec(memory_space=pl.ANY), vmem],
+        in_specs=[pl.BlockSpec(memory_space=pl.ANY)] + [vmem] * len(given),
         out_specs=vmem,
         scratch_shapes=[
             pltpu.VMEM((3, chans, tokens), jnp.bfloat16),
@@ -424,9 +445,9 @@
             pltpu.SemaphoreType.DMA((steps, groups)),
         ],
         compiler_params=pltpu.CompilerParams(
-            collective_id=0, has_side_effects=True, vmem_limit_bytes=48 * 1024 * 1024
+            collective_id=0, has_side_effects=True, vmem_limit_bytes=62 * 1024 * 1024
         ),
-    )(qkv[0], given)
+    )(qkv[0], *given)
     return out[None]
 
 

time: 43.8 us -> 42.2 us (0.963)
  other arithmetic: 1.49 us -> 0 us
  local copies, waits for them, and re-layouts: 3.69 us -> 2.26 us
  Pallas kernels: 38.3 us -> 39.7 us
    concatenate x2 -> x0, other arithmetic: 1.49 us -> none  [the longest x1 0.76 us: local_pack(): jnp.concatenate([taps.reshape(9, width), bias[None], jnp.zeros((rows * dp...]
    pallas_call x1, Pallas kernels: 38.3 us -> 39.7 us  [per_device(): pl.pallas_call(functools.partial(mixer_kernel, dp, ctx, blocks, tokens, i...]
    reshape x2 -> x0, local copies, waits for them, and re-layouts: 0.75 us -> none  [the longest x1 0.75 us: local_pack(): taps.reshape(9, width)]
    unnamed x3 -> x1, local copies, waits for them, and re-layouts: 2.86 us -> 2.26 us
where the time goes in v4:
time: 42.2 us; the launch traced here: 41.9 us
  Pallas kernels  39.7 us (94%)
  local copies, waits for them, and re-layouts  2.26 us (5%)
    pallas_call x1, Pallas kernels, per_device(): pl.pallas_call(functools.partial(mixer_kernel, dp, ctx, blocks, tokens, i...  39.7 us
    unnamed x1, local copies, waits for them, and re-layouts  2.26 us

profile of v4, /device:TPU:24, one launch (start us, length us, event | category | flops | bytes accessed | tf_op | source)
XLA Modules:
  0.0 41.9 jit_solution(564923443864864631)
XLA Ops:
  0.0 39.7 %shard_map.55 = bf16[4096,128]{1,0:T(8,128)(2,1)} custom-call(bf16[3,4096,128]{2,1,0:T(8,128)(2,1)} %bitcast.4, f32[4,512]{1,0:T(4,128)} %refs_1_.1, f32[4,512]{1,0:T(4,128)} %refs_2_.1, f32[3,3,512]{2,1,0:T(4,128)} %refs_3_.1, f32[1,512]{1,0:T(1,128)} %bitcast.5), custom_call_target="tpu_custom_call" | custom-call | tf_op jit(solution)/shard_map/pallas_call | solution.py:420
  39.7 2.3 %copy.7 = bf16[1,4096,128]{2,1,0:T(8,128)(2,1)} copy(bf16[1,4096,128]{2,1,0:T(8,128)(2,1)} %bitcast.3) | data formatting | bytes 2097152

commit v5 on v4

--- a/solution.py
+++ b/solution.py
@@ -171,7 +171,6 @@
         fetch(group).wait()
         to_tokens(eye, raw.at[1], k_s, blocks, group, tokens)
         to_tokens(eye, raw.at[2], v_s, blocks, group, tokens)
-        to_tokens(eye, raw.at[0], q_s, blocks, group, tokens)
         if inside and group == groups // 2 - 1:
             lax.fori_loop(1, ctx, pass_on, 0)
 
@@ -189,8 +188,17 @@
 
     @pl.when(me + 1 < ctx)
     def _():
-        for copy in ends:
+        for copy in ends[1:]:
             copy.start()
+
+    for group in range(groups):
+        if inside and group == groups // 2:
+            lax.fori_loop(0, ctx, pass_far, 0)
+        to_tokens(eye, raw.at[0], q_s, blocks, group, tokens)
+
+    @pl.when(me + 1 < ctx)
+    def _():
+        ends[0].start()
 
     @pl.when(me == 0)
     def _():
@@ -210,7 +218,6 @@
             came[s] = jnp.zeros_like(came[s])
 
     if inside:
-        lax.fori_loop(0, ctx, pass_far, 0)
         lax.fori_loop(0, ctx, arrive, 0)
 
         def place(d, _):
@@ -445,7 +452,7 @@
             pltpu.SemaphoreType.DMA((steps, groups)),
         ],
         compiler_params=pltpu.CompilerParams(
-            collective_id=0, has_side_effects=True, vmem_limit_bytes=62 * 1024 * 1024
+            collective_id=0, has_side_effects=True, vmem_limit_bytes=61 * 1024 * 1024
         ),
     )(qkv[0], *given)
     return out[None]

time: 42.2 us -> 43.7 us (1.036)
  Pallas kernels: 39.7 us -> 41.2 us
    pallas_call x1, Pallas kernels: 39.7 us -> 41.2 us  [per_device(): pl.pallas_call(functools.partial(mixer_kernel, dp, ctx, blocks, tokens, i...]
where the time goes in v5:
time: 43.7 us; the launch traced here: 43.4 us
  Pallas kernels  41.2 us (94%)
  local copies, waits for them, and re-layouts  2.26 us (5%)
    pallas_call x1, Pallas kernels, per_device(): pl.pallas_call(functools.partial(mixer_kernel, dp, ctx, blocks, tokens, i...  41.2 us
    unnamed x1, local copies, waits for them, and re-layouts  2.26 us

profile of v5, /device:TPU:24, one launch (start us, length us, event | category | flops | bytes accessed | tf_op | source)
XLA Modules:
  0.0 43.4 jit_solution(8959923121533088139)
XLA Ops:
  0.0 41.2 %shard_map.55 = bf16[4096,128]{1,0:T(8,128)(2,1)} custom-call(bf16[3,4096,128]{2,1,0:T(8,128)(2,1)} %bitcast.4, f32[4,512]{1,0:T(4,128)} %refs_1_.1, f32[4,512]{1,0:T(4,128)} %refs_2_.1, f32[3,3,512]{2,1,0:T(4,128)} %refs_3_.1, f32[1,512]{1,0:T(1,128)} %bitcast.5), custom_call_target="tpu_custom_call" | custom-call | tf_op jit(solution)/shard_map/pallas_call | solution.py:427
  41.2 2.3 %copy.7 = bf16[1,4096,128]{2,1,0:T(8,128)(2,1)} copy(bf16[1,4096,128]{2,1,0:T(8,128)(2,1)} %bitcast.3) | data formatting | bytes 2097152
